TPU v7x, 128 devices: a whole 4x4x4 slice. The times are simulated.
128 devices in a mesh: dp: 8 (over z, core), ctx: 16 (over y, x).
Axes of the slice: x: 4, y: 4, z: 4, core: 2. Of those that a mesh axis runs over, the one named last changes fastest.
Arguments:
- tokens: bfloat16 [24576, 1024], P(('dp', 'ctx')), may hold values from -55 to 55
- segments: int32 [8, 3072], P('dp', 'ctx'), may hold values from 0 to 7, never falling along the last dimension, each value on 1 to 1536 neighbouring positions
- w_in: bfloat16 [1024, 4096], replicated, may hold values from -0.1875 to 0.1875
- w_out: bfloat16 [1024, 1024], replicated, may hold values from -0.1875 to 0.1875
- grad_out: bfloat16 [24576, 1024], P(('dp', 'ctx')), may hold values from -24 to 24
Outputs:
- layer_out: bfloat16 [24576, 1024], P(('dp', 'ctx'))
- grad_tokens: bfloat16 [24576, 1024], P(('dp', 'ctx'))
- out_grad: float32 [1024, 1024], P(('dp', 'ctx'))
Inputs may be any that keep to these rules, and one draw needn't show every extreme that they name: `segments`: along each stream's stored rows the history number never falls; each of the 8 histories holds 1 to 1536 events, one exactly 1536.
All inputs are finite; a program needn't handle non-finite values.
Results may differ from a plain program's by a relative error of at most 0.008.
Values may be sent and summed in bfloat16 or wider, within the bound.
A program may use at most 128 MiB of HBM per device.

v0:
```python
import jax
import jax.numpy as jnp
from jax import lax
from jax.sharding import PartitionSpec as P

HEADS = 8
EPS = 1e-05


def silu_grad(value):
    sigmoid_v = jax.nn.sigmoid(value)
    return sigmoid_v * (1.0 + value * (1.0 - sigmoid_v))


def norm_rows(matrix):
    average = jnp.mean(matrix, axis=-1, keepdims=True)
    centred = matrix - average
    inverse = lax.rsqrt(jnp.mean(centred * centred, axis=-1, keepdims=True) + EPS)
    return (centred * inverse, inverse)


def norm_back(gradient, normed, inverse):
    first = jnp.mean(gradient, axis=-1, keepdims=True)
    second = jnp.mean(gradient * normed, axis=-1, keepdims=True)
    return (gradient - first - normed * second) * inverse


def head_major(matrix):
    return matrix.reshape(matrix.shape[0], HEADS, matrix.shape[1] // HEADS).transpose(1, 0, 2)


def row_major(stacked):
    return stacked.transpose(1, 0, 2).reshape(stacked.shape[1], stacked.shape[0] * stacked.shape[2])


def place_of(stored, own_rows, ctx_count):
    block = stored // own_rows
    inner = stored % own_rows
    half = own_rows // 2
    return jnp.where(
        inner < half, block * half + inner, (2 * ctx_count - 1 - block) * half + inner - half
    )


def on_device(tokens, segments, w_in, w_out, grad_out):
    own_rows, model_width = tokens.shape
    ctx_count = lax.axis_size("ctx")
    score_scale = (model_width // HEADS) ** (-0.5)
    device_pos = lax.axis_index("ctx")
    positions = place_of(
        device_pos * own_rows + jnp.arange(own_rows, dtype=jnp.int32), own_rows, ctx_count
    )
    history = segments[0]
    xfloat = tokens.astype(jnp.float32)
    normed, inv_x = norm_rows(xfloat)
    normed_b = normed.astype(jnp.bfloat16)
    preact = jnp.dot(normed_b, w_in, preferred_element_type=jnp.float32)
    act = jax.nn.silu(preact).astype(jnp.bfloat16)
    gate_u = act[:, :model_width]
    own_values = act[:, model_width : 2 * model_width]
    queries = act[:, 2 * model_width : 3 * model_width]
    own_keys = act[:, 3 * model_width :]
    keys_all, values_all, history_all = (
        lax.all_gather(own_keys, "ctx", axis=0, tiled=True),
        lax.all_gather(own_values, "ctx", axis=0, tiled=True),
        lax.all_gather(history, "ctx", axis=0, tiled=True),
    )
    places_all = place_of(jnp.arange(keys_all.shape[0], dtype=jnp.int32), own_rows, ctx_count)
    visible = (history[:, None] == history_all[None, :]) & (
        positions[:, None] >= places_all[None, :]
    )
    query_h = head_major(queries)
    keys_h = head_major(keys_all)
    values_h = head_major(values_all)

    def forward_head(operands):
        one_q, one_k, one_v = operands
        scores = jnp.dot(one_q, one_k.T, preferred_element_type=jnp.float32) * score_scale
        weights = jnp.where(visible, jax.nn.silu(scores), 0.0).astype(jnp.bfloat16)
        return jnp.dot(weights, one_v, preferred_element_type=jnp.float32)

    mixed = row_major(lax.map(forward_head, (query_h, keys_h, values_h)))
    mixed_n, inv_o = norm_rows(mixed)
    gated = (mixed_n * gate_u.astype(jnp.float32)).astype(jnp.bfloat16)
    layer_out = (jnp.dot(gated, w_out, preferred_element_type=jnp.float32) + xfloat).astype(
        jnp.bfloat16
    )
    total_rows = own_rows * lax.axis_size(("dp", "ctx"))
    out_grad = lax.psum_scatter(
        jnp.einsum("re,rd->ed", grad_out, gated, preferred_element_type=jnp.float32),
        ("dp", "ctx"),
        scatter_dimension=0,
        tiled=True,
    ) * total_rows ** (-0.5)
    grad_gated = jnp.einsum("re,de->rd", grad_out, w_out, preferred_element_type=jnp.float32)
    grad_u = grad_gated * mixed_n
    grad_norm = grad_gated * gate_u.astype(jnp.float32)
    grad_mixed = norm_back(grad_norm, mixed_n, inv_o).astype(jnp.bfloat16)
    grad_h = head_major(grad_mixed)

    def query_head(operands):
        one_q, one_k, one_v, one_g = operands
        scores = jnp.dot(one_q, one_k.T, preferred_element_type=jnp.float32) * score_scale
        grad_weights = jnp.dot(one_g, one_v.T, preferred_element_type=jnp.float32)
        grad_scores = (
            jnp.where(visible, grad_weights * silu_grad(scores), 0.0) * score_scale
        ).astype(jnp.bfloat16)
        return jnp.dot(grad_scores, one_k, preferred_element_type=jnp.float32)

    grad_queries = row_major(lax.map(query_head, (query_h, keys_h, values_h, grad_h)))
    own_keys_h = head_major(own_keys)
    own_values_h = head_major(own_values)
    piece_q = lax.all_gather(queries, "ctx", axis=0, tiled=True)
    piece_grad = lax.all_gather(grad_mixed, "ctx", axis=0, tiled=True)
    piece_hist = lax.all_gather(history, "ctx", axis=0, tiled=True)
    row_count = piece_q.shape[0]
    piece_pos = place_of(jnp.arange(row_count, dtype=jnp.int32), own_rows, ctx_count)
    piece_visible = (piece_hist[:, None] == history[None, :]) & (
        piece_pos[:, None] >= positions[None, :]
    )

    def key_head(operands):
        one_q, one_g, one_k, one_v = operands
        scores = jnp.dot(one_q, one_k.T, preferred_element_type=jnp.float32) * score_scale
        weights = jnp.where(piece_visible, jax.nn.silu(scores), 0.0).astype(jnp.bfloat16)
        grad_weights = jnp.dot(one_g, one_v.T, preferred_element_type=jnp.float32)
        grad_scores = (
            jnp.where(piece_visible, grad_weights * silu_grad(scores), 0.0) * score_scale
        ).astype(jnp.bfloat16)
        key_part = jnp.dot(grad_scores.T, one_q, preferred_element_type=jnp.float32)
        value_part = jnp.dot(weights.T, one_g, preferred_element_type=jnp.float32)
        return (key_part, value_part)

    key_part, value_part = lax.map(
        key_head, (head_major(piece_q), head_major(piece_grad), own_keys_h, own_values_h)
    )
    grad_keys = row_major(key_part)
    grad_values = row_major(value_part)
    grad_all = jnp.concatenate([grad_u, grad_values, grad_queries, grad_keys], axis=1)
    grad_pre = (grad_all * silu_grad(preact)).astype(jnp.bfloat16)
    grad_rows = jnp.einsum("rf,df->rd", grad_pre, w_in, preferred_element_type=jnp.float32)
    grad_tokens = (grad_out.astype(jnp.float32) + norm_back(grad_rows, normed, inv_x)).astype(
        jnp.bfloat16
    )
    return (layer_out, grad_tokens, out_grad)


def solution(mesh):
    return jax.shard_map(
        on_device,
        mesh=mesh,
        in_specs=(P(("dp", "ctx"), None), P("dp", "ctx"), P(), P(), P(("dp", "ctx"), None)),
        out_specs=(P(("dp", "ctx"), None), P(("dp", "ctx"), None), P(("dp", "ctx"), None)),
        check_vma=False,
    )
```

profile of v0, /device:TPU:1, one launch (start us, length us, event | category | flops | bytes accessed | tf_op | source)
XLA Modules:
  0.0 1003.1 jit_solution(6318163071438569828)
XLA Ops:
  9.8 7.2 multiply_convert_fusion
  23.6 62.2 %all-reduce = s32[3072]{0:T(1024)S(1)} all-reduce(s32[3072]{0:T(1024)S(1)} %dynamic-update-slice), channel_id=2, replica_groups=mesh['dp'=8,'ctx'=16] {'ctx'}, use_global_device_ids=true, to_apply=%add | all-reduce | flops 3072 | bytes 24576 | tf_op jit(solution)/shard_map/all_gather | solution.py:66
  85.8 6.6 bitcast_bitcast_fusion.2
  92.4 55.4 %all-gather.6.cloned.1.call-done = bf16[3072,1024]{1,0:T(8,128)(2,1)} async-done(((bf16[192,1024]{1,0:T(8,128)(2,1)}), bf16[3072,1024]{1,0:T(8,128)(2,1)}) %all-gather.6.cloned.1.call-update) | async-done | bytes 6291472 | tf_op jit(solution)/shard_map/all_gather | solution.py:64
  147.8 6.5 bitcast_bitcast_fusion.3
  154.4 22.1 %while.35 = (s32[]{:T(128)}, f32[8,192,128]{2,1,0:T(8,128)S(1)}, bf16[8,192,128]{2,1,0:T(8,128)(2,1)}, bf16[8,3072,128]{2,1,0:T(8,128)(2,1)}, bf16[8,3072,128]{2...) while((s32[]{:T(128)}, f32[8,192,128]{2,1,0:T(8,128)S(1)}, ...), condition=%wide.region_3.4_spmd.clone, body=%wide.region_2.3_spmd.clone.sunk | while | flops 307888128 | bytes 1749093 | solution.py:82
  154.4 2.8 fusion.188
  157.2 2.7 fusion.188
  159.9 2.8 fusion.188
  162.7 2.7 fusion.188
  165.4 2.7 fusion.188
  168.2 2.7 fusion.188
  171.0 2.7 fusion.188
  173.7 2.7 fusion.188
  176.8 3.8 convolution_bitcast_fusion
  180.6 5.4 copy.34
  195.5 58.9 %while.37 = (s32[]{:T(128)}, f32[8,192,128]{2,1,0:T(8,128)}, bf16[8,192,128]{2,1,0:T(8,128)(2,1)}, bf16[8,3072,128]{2,1,0:T(8,128)(2,1)}, bf16[8,192,128]{2,1,0:...) while((s32[]{:T(128)}, f32[8,192,128]{2,1,0:T(8,128)}, ...), condition=%wide.region_11.12_spmd.clone, body=%wide.region_10.11_spmd.clone.sunk | while | flops 461832192 | bytes 7303789 | solution.py:110
  195.5 3.1 convolution_multiply_fusion.8
  198.6 4.4 fusion.202
  202.9 3.1 convolution_multiply_fusion.8
  206.0 4.3 fusion.202
  210.3 3.0 convolution_multiply_fusion.8
  213.3 4.3 fusion.202
  217.6 3.0 convolution_multiply_fusion.8
  220.7 4.3 fusion.202
  225.0 3.0 convolution_multiply_fusion.8
  228.0 4.3 fusion.202
  232.3 3.0 convolution_multiply_fusion.8
  235.4 4.3 fusion.202
  239.7 3.0 convolution_multiply_fusion.8
  242.7 4.3 fusion.202
  247.0 3.0 convolution_multiply_fusion.8
  250.1 4.3 fusion.202
  258.9 6.6 bitcast_bitcast_fusion
  265.5 559.4 %reduce-scatter.4.cloned.1.call-done = f32[8,1024]{1,0:T(8,128)} async-done(((f32[1024,1024]{1,0:T(8,128)}), f32[8,1024]{1,0:T(8,128)}) %reduce-scatter.4.cloned.1.call-update) | async-done | bytes 32784
  826.6 87.1 %all-gather.10.cloned.1.call-done = bf16[3072,1024]{1,0:T(8,128)(2,1)} async-done(((bf16[192,1024]{1,0:T(8,128)(2,1)}), bf16[3072,1024]{1,0:T(8,128)(2,1)}) %all-gather.10.cloned.1.call-update) | async-done | bytes 6291472 | tf_op jit(solution)/shard_map/all_gather | solution.py:114
  913.7 6.6 bitcast_bitcast_fusion.1
  922.3 63.1 %while.36 = (s32[]{:T(128)}, f32[8,192,128]{2,1,0:T(8,128)}, f32[8,192,128]{2,1,0:T(8,128)}, bf16[8,3072,128]{2,1,0:T(8,128)(2,1)}, bf16[8,192,128]{2,1,0:T(8,12...) while((s32[]{:T(128)}, f32[8,192,128]{2,1,0:T(8,128)}, ...), condition=%wide.region_9.10_spmd.clone, body=%wide.region_8.9_spmd.clone.sunk | while | flops 618135552 | bytes 10574965 | solution.py:134
  923.9 3.6 fusion.195
  931.8 3.6 fusion.195
  939.6 3.6 fusion.195
  947.6 3.6 fusion.195
  955.4 3.6 fusion.195
  963.3 3.6 fusion.195
  966.9 2.7 fusion.196
  971.2 3.6 fusion.195
  979.1 3.6 fusion.195
  988.0 7.4 fusion.148
  (83 shorter events, 61.7 us)
Async XLA Ops:
  7.2 179.0 %copy-start = (bf16[1024,1024]{1,0:T(8,128)(2,1)S(1)}, bf16[1024,1024]{1,0:T(8,128)(2,1)}, u32[]{:S(2)}) copy-start(bf16[1024,1024]{1,0:T(8,128)(2,1)} %param.14) | copy-start | bytes 6291460
  7.2 78.6 %all-gather.8.cloned.1.call-start = ((), (), s32[]{:S(2)}) async-start(), calls=%async_computation.2 | async-start | bytes 6684672 | tf_op jit(solution)/shard_map/all_gather | solution.py:65
  16.9 1.1 copy-start.3
  18.1 3.8 copy-start.10
  18.1 5.2 copy-start.9
  19.5 128.3 %all-gather.6.cloned.1.call-start = ((), (), s32[]{:S(2)}) async-start(), calls=%async_computation.1 | async-start | bytes 6684672 | tf_op jit(solution)/shard_map/all_gather | solution.py:64
  20.3 238.6 %all-gather.12.cloned.1.call-start = ((), (), s32[]{:S(2)}) async-start(), calls=%async_computation.4 | async-start | bytes 6684672 | tf_op jit(solution)/shard_map/all_gather | solution.py:113
  21.0 803.8 %reduce-scatter.4.cloned.1.call-start = ((), (), s32[]{:S(2)}) async-start(), calls=%async_computation.5 | async-start | bytes 4227072
  154.4 22.5 %copy-start.4 = (bf16[192,1024]{1,0:T(8,128)(2,1)S(1)}, bf16[192,1024]{1,0:T(8,128)(2,1)}, u32[]{:S(2)}) copy-start(bf16[192,1024]{1,0:T(8,128)(2,1)} %param.15) | copy-start | bytes 1179652
  186.1 727.7 %all-gather.10.cloned.1.call-start = ((), (), s32[]{:S(2)}) async-start(), calls=%async_computation.3 | async-start | bytes 6684672 | tf_op jit(solution)/shard_map/all_gather | solution.py:114
  188.2 2.4 copy-start.6
  195.5 61.0 %copy-start.2 = (bf16[192,1024]{1,0:T(8,128)(2,1)S(1)}, bf16[192,1024]{1,0:T(8,128)(2,1)}, u32[]{:S(2)}) copy-start(bf16[192,1024]{1,0:T(8,128)(2,1)} %param.11) | copy-start | bytes 1179652
  985.4 2.6 copy-start.7
  985.4 2.6 copy-start.8
  987.9 7.5 copy-start.5
  988.0 8.6 copy-start.1
Sparse Core Ops, SparseCore 0:
  19.6 65.2 all-gather.7
  87.0 60.7 all-gather.5
  149.9 60.8 all-gather.11
  213.0 611.7 reduce-scatter.3
  827.0 86.6 all-gather.9
where the time goes:
time: 1010 us; the launch traced here: 1000 us
  waiting for transfers between devices  703 us (70%)
  matrix products  167 us (17%)
  blocking collectives  62.2 us (6%)
  local copies, waits for them, and re-layouts  49.4 us (5%)
  between operations  14.7 us (1%)
    unnamed x6, waiting for transfers between devices  561 us
    all_gather x1, waiting for transfers between devices, on_device(): piece_grad = lax.all_gather(grad_mixed, 'ctx', axis=0, tiled=True)  87.1 us
    all_gather x1, blocking collectives, on_device(): lax.all_gather(history, 'ctx', axis=0, tiled=True)  62.2 us
    all_gather x1, waiting for transfers between devices, on_device(): lax.all_gather(own_keys, 'ctx', axis=0, tiled=True)  55.4 us
    dot_general x8, matrix products, query_head(): return jnp.dot(grad_scores, one_k, preferred_element_type=jnp.float32)  34.5 us
    transpose x6, local copies, waits for them, and re-layouts, head_major(): matrix.reshape(matrix.shape[0], HEADS, matrix.shape[1] // HEADS)  30.2 us
    dot_general x8, matrix products, key_head(): key_part = jnp.dot(grad_scores.T, one_q, preferred_element_type=jnp.float32)  28.8 us
    dot_general x8, matrix products, query_head(): jnp.dot(one_q, one_k.T, preferred_element_type=jnp.float32) * score_scale  24.4 us
  transfers between devices with their start and end apart: 5, of which 3 were waited for; matrix products, arithmetic and copies ran while one was open for 13% of the time, Pallas kernels for 0%

commit v1 on v0

--- a/solution.py
+++ b/solution.py
@@ -2,6 +2,7 @@
 import jax.numpy as jnp
 from jax import lax
 from jax.sharding import PartitionSpec as P
+from jax.lax import all_gather
 
 HEADS = 8
 EPS = 1e-05
@@ -110,8 +111,8 @@
     grad_queries = row_major(lax.map(query_head, (query_h, keys_h, values_h, grad_h)))
     own_keys_h = head_major(own_keys)
     own_values_h = head_major(own_values)
-    piece_q = lax.all_gather(queries, "ctx", axis=0, tiled=True)
-    piece_grad = lax.all_gather(grad_mixed, "ctx", axis=0, tiled=True)
+    upper = all_gather(jnp.concatenate([queries, grad_mixed], axis=1), "ctx", axis=0, tiled=True)
+    piece_q, piece_grad = jnp.split(upper, [queries.shape[1]], axis=1)
     piece_hist = lax.all_gather(history, "ctx", axis=0, tiled=True)
     row_count = piece_q.shape[0]
     piece_pos = place_of(jnp.arange(row_count, dtype=jnp.int32), own_rows, ctx_count)

time: 1010 us -> 1020 us (level)
  waiting for transfers between devices: 703 us -> 714 us
    all_gather x2 -> x1, waiting for transfers between devices: 87.1 us -> 116 us  [on_device(): all_gather(jnp.concatenate([queries, grad_mixed], axis=1), 'ctx', axis=0,...]
    unnamed x6 -> x5, waiting for transfers between devices: 561 us -> 541 us
    transpose x6 -> x4, local copies, waits for them, and re-layouts: 30.2 us -> 16 us  [head_major(): matrix.reshape(matrix.shape[0], HEADS, matrix.shape[1] // HEADS)]
  transfers between devices with their start and end apart: 5 -> 4, of which waited for: 3 -> 3; matrix products, arithmetic and copies ran while one was open for 13% -> 8% of each run, Pallas kernels for 0% -> 0%
where the time goes in v1:
time: 1020 us; the launch traced here: 1010 us
  waiting for transfers between devices  714 us (70%)
  matrix products  166 us (16%)
  blocking collectives  62.1 us (6%)
  local copies, waits for them, and re-layouts  49.1 us (5%)
  between operations  14.5 us (1%)
    unnamed x5, waiting for transfers between devices  541 us
    all_gather x1, waiting for transfers between devices, on_device(): all_gather(jnp.concatenate([queries, grad_mixed], axis=1), 'ctx', axis=0,...  116 us
    all_gather x1, blocking collectives, on_device(): lax.all_gather(history, 'ctx', axis=0, tiled=True)  62.1 us
    all_gather x1, waiting for transfers between devices, on_device(): lax.all_gather(own_keys, 'ctx', axis=0, tiled=True)  56.3 us
    dot_general x8, matrix products, query_head(): return jnp.dot(grad_scores, one_k, preferred_element_type=jnp.float32)  34.4 us
    dot_general x8, matrix products, key_head(): key_part = jnp.dot(grad_scores.T, one_q, preferred_element_type=jnp.float32)  28.8 us
    dot_general x8, matrix products, query_head(): jnp.dot(one_q, one_k.T, preferred_element_type=jnp.float32) * score_scale  24.3 us
    dot_general x8, matrix products, forward_head(): return jnp.dot(weights, one_v, preferred_element_type=jnp.float32)  21.8 us
  transfers between devices with their start and end apart: 4, of which 3 were waited for; matrix products, arithmetic and copies ran while one was open for 8% of the time, Pallas kernels for 0%

profile of v1, /device:TPU:1, one launch (start us, length us, event | category | flops | bytes accessed | tf_op | source)
XLA Modules:
  0.0 1013.6 jit_solution(7244850895848542016)
XLA Ops:
  9.8 7.2 multiply_convert_fusion
  22.6 62.1 %all-reduce = s32[3072]{0:T(1024)S(1)} all-reduce(s32[3072]{0:T(1024)S(1)} %dynamic-update-slice), channel_id=2, replica_groups=mesh['dp'=8,'ctx'=16] {'ctx'}, use_global_device_ids=true, to_apply=%add | all-reduce | flops 3072 | bytes 24576 | tf_op jit(solution)/shard_map/all_gather | solution.py:67
  84.8 6.5 bitcast_bitcast_fusion.2
  91.3 56.3 %all-gather.5.cloned.1.call-done = bf16[3072,1024]{1,0:T(8,128)(2,1)} async-done(((bf16[192,1024]{1,0:T(8,128)(2,1)}), bf16[3072,1024]{1,0:T(8,128)(2,1)}) %all-gather.5.cloned.1.call-update) | async-done | bytes 6291472 | tf_op jit(solution)/shard_map/all_gather | solution.py:65
  147.5 6.5 bitcast_bitcast_fusion.3
  154.1 21.9 %while.35 = (s32[]{:T(128)}, f32[8,192,128]{2,1,0:T(8,128)S(1)}, bf16[8,192,128]{2,1,0:T(8,128)(2,1)}, bf16[8,3072,128]{2,1,0:T(8,128)(2,1)}, bf16[8,3072,128]{2...) while((s32[]{:T(128)}, f32[8,192,128]{2,1,0:T(8,128)S(1)}, ...), condition=%wide.region_3.4_spmd.clone, body=%wide.region_2.3_spmd.clone.sunk | while | flops 307888128 | bytes 1749093 | solution.py:83
  154.1 2.8 fusion.186
  156.9 2.7 fusion.186
  159.7 2.7 fusion.186
  162.4 2.7 fusion.186
  165.1 2.7 fusion.186
  167.9 2.7 fusion.186
  170.6 2.7 fusion.186
  173.3 2.7 fusion.186
  176.5 3.8 convolution_bitcast_fusion
  180.2 5.3 copy.34
  194.9 58.7 %while.37 = (s32[]{:T(128)}, f32[8,192,128]{2,1,0:T(8,128)}, bf16[8,192,128]{2,1,0:T(8,128)(2,1)}, bf16[8,3072,128]{2,1,0:T(8,128)(2,1)}, bf16[8,192,128]{2,1,0:...) while((s32[]{:T(128)}, f32[8,192,128]{2,1,0:T(8,128)}, ...), condition=%wide.region_11.12_spmd.clone, body=%wide.region_10.11_spmd.clone.sunk | while | flops 461832192 | bytes 7303789 | solution.py:111
  194.9 3.1 convolution_multiply_fusion.8
  198.0 4.3 fusion.200
  202.3 3.0 convolution_multiply_fusion.8
  205.3 4.3 fusion.200
  209.6 3.0 convolution_multiply_fusion.8
  212.6 4.3 fusion.200
  216.9 3.0 convolution_multiply_fusion.8
  219.9 4.3 fusion.200
  224.2 3.0 convolution_multiply_fusion.8
  227.3 4.3 fusion.200
  231.6 3.0 convolution_multiply_fusion.8
  234.6 4.3 fusion.200
  238.9 3.0 convolution_multiply_fusion.8
  242.0 4.3 fusion.200
  246.3 3.0 convolution_multiply_fusion.8
  249.3 4.3 fusion.200
  258.1 540.5 %reduce-scatter.4.cloned.1.call-done = f32[8,1024]{1,0:T(8,128)} async-done(((f32[1024,1024]{1,0:T(8,128)}), f32[8,1024]{1,0:T(8,128)}) %reduce-scatter.4.cloned.1.call-update) | async-done | bytes 32784
  800.4 116.3 %all-gather.9.cloned.1.call-done = bf16[3072,2048]{1,0:T(8,128)(2,1)} async-done(((bf16[192,2048]{1,0:T(8,128)(2,1)}), bf16[3072,2048]{1,0:T(8,128)(2,1)}) %all-gather.9.cloned.1.call-update) | async-done | bytes 12582928 | tf_op jit(solution)/shard_map/all_gather | solution.py:114
  916.7 6.5 slice_bitcast_fusion
  923.2 3.8 copy.72
  927.0 3.8 copy.73
  932.8 63.1 %while.36 = (s32[]{:T(128)}, f32[8,192,128]{2,1,0:T(8,128)}, f32[8,192,128]{2,1,0:T(8,128)}, bf16[8,3072,128]{2,1,0:T(8,128)(2,1)}, bf16[8,192,128]{2,1,0:T(8,12...) while((s32[]{:T(128)}, f32[8,192,128]{2,1,0:T(8,128)}, ...), condition=%wide.region_9.10_spmd.clone, body=%wide.region_8.9_spmd.clone.sunk | while | flops 618135552 | bytes 10574965 | solution.py:135
  934.4 3.6 fusion.193
  942.3 3.6 fusion.193
  950.2 3.6 fusion.193
  958.0 3.6 fusion.193
  965.9 3.6 fusion.193
  973.8 3.6 fusion.193
  981.7 3.6 fusion.193
  989.6 3.6 fusion.193
  998.5 7.4 fusion.148
  (82 shorter events, 63.5 us)
Async XLA Ops:
  7.2 178.5 %copy-start = (bf16[1024,1024]{1,0:T(8,128)(2,1)S(1)}, bf16[1024,1024]{1,0:T(8,128)(2,1)}, u32[]{:S(2)}) copy-start(bf16[1024,1024]{1,0:T(8,128)(2,1)} %param.14) | copy-start | bytes 6291460
  7.2 77.6 %all-gather.7.cloned.1.call-start = ((), (), s32[]{:S(2)}) async-start(), calls=%async_computation.2 | async-start | bytes 6684672 | tf_op jit(solution)/shard_map/all_gather | solution.py:66
  16.9 1.1 copy-start.3
  18.1 3.1 copy-start.10
  18.1 4.2 copy-start.9
  19.5 128.0 %all-gather.5.cloned.1.call-start = ((), (), s32[]{:S(2)}) async-start(), calls=%async_computation.1 | async-start | bytes 6684672 | tf_op jit(solution)/shard_map/all_gather | solution.py:65
  20.3 778.4 %reduce-scatter.4.cloned.1.call-start = ((), (), s32[]{:S(2)}) async-start(), calls=%async_computation.4 | async-start | bytes 4227072
  154.1 22.3 %copy-start.4 = (bf16[192,1024]{1,0:T(8,128)(2,1)S(1)}, bf16[192,1024]{1,0:T(8,128)(2,1)}, u32[]{:S(2)}) copy-start(bf16[192,1024]{1,0:T(8,128)(2,1)} %param.15) | copy-start | bytes 1179652
  185.6 731.1 %all-gather.9.cloned.1.call-start = ((), (), s32[]{:S(2)}) async-start(), calls=%async_computation.3 | async-start | bytes 13369344 | tf_op jit(solution)/shard_map/all_gather | solution.py:114
  187.7 2.3 copy-start.6
  194.9 60.8 %copy-start.2 = (bf16[192,1024]{1,0:T(8,128)(2,1)S(1)}, bf16[192,1024]{1,0:T(8,128)(2,1)}, u32[]{:S(2)}) copy-start(bf16[192,1024]{1,0:T(8,128)(2,1)} %param.11) | copy-start | bytes 1179652
  995.9 2.6 copy-start.7
  995.9 2.6 copy-start.8
  998.5 7.5 copy-start.5
  998.5 8.6 copy-start.1
Sparse Core Ops, SparseCore 0:
  19.6 64.8 all-gather.6
  86.7 60.8 all-gather.4
  185.7 612.8 reduce-scatter.3
  800.8 115.8 all-gather.8
